TPU v7x, 256 devices: a whole 4x4x8 slice. The times are simulated.
256 devices in a mesh: row: 8 (over y, x_hi), col: 32 (over x_lo, z, core).
Axes of the slice: x: 4 (x_hi: 2, x_lo: 2; x = x_hi * 2 + x_lo), y: 4, z: 8, core: 2. Of those that a mesh axis runs over, the one named last changes fastest.
Arguments:
- spectra: bfloat16 [512, 2, 128, 4096], P('col', None, None, 'row'), may hold values from -150 to 150
- kept_bins: int32 [24], replicated, may hold values from 0 to 127, as said below
- keep_mask: int32 [512], P('col'), may hold values 0 or 1
Outputs:
- stack: bfloat16 [24, 2, 4096, 4096], P(None, None, 'row', 'col')
Inputs may be any that keep to these rules, and one draw needn't show every extreme that they name: `kept_bins`: 24 distinct bins.
All inputs are finite; a program needn't handle non-finite values. No bound on the sum of `keep_mask` on one device may be relied on, other than what follows from the above.
Results may differ from a plain program's by a relative error of at most 0.0057.
Values may be sent and summed in bfloat16 or wider, within the bound.
A program may use at most 192 MiB of HBM per device.

v0:
```python
import math

import jax
import jax.numpy as jnp
from jax import lax
from jax.sharding import PartitionSpec as P

CHAN_COL = 128


def spread(block, axis, source):
    block = jnp.where(lax.axis_index(axis) == source, block, jnp.zeros_like(block))
    return lax.psum(block, axis)


def whiten(spectra, kept_bins, keep_mask):
    raw = spectra.astype(jnp.float32)
    power = jnp.mean(raw * raw, axis=(1, 2))
    factor = keep_mask.astype(jnp.float32)[:, None] / jnp.sqrt(power + 1e-06)
    band = spectra.shape[2]
    onehot = (kept_bins[:, None] == jnp.arange(band, dtype=jnp.int32)[None, :]).astype(jnp.bfloat16)
    picked = jnp.einsum("fb,wpbc->fpwc", onehot, spectra, preferred_element_type=jnp.float32)
    return (picked * factor[None, None]).astype(jnp.bfloat16)


def cross_block(left_block, right_block):
    bins = left_block.shape[0]
    depth = 2 * left_block.shape[2]
    left = left_block.reshape(bins, depth, left_block.shape[3])
    turned = jnp.concatenate([left_block[:, 1], -left_block[:, 0]], 1)
    right = right_block.reshape(bins, depth, right_block.shape[3])
    dims = (((1,), (1,)), ((0,), (0,)))
    real_out = lax.dot_general(left, right, dims, preferred_element_type=jnp.float32)
    imag_out = lax.dot_general(turned, right, dims, preferred_element_type=jnp.float32)
    return jnp.stack([real_out, imag_out], 1)


def per_device(spectra, kept_bins, keep_mask):
    white = whiten(spectra, kept_bins, keep_mask)
    row_width = white.shape[3]
    col_index = lax.axis_index("col")
    owner = col_index * CHAN_COL // row_width
    offset = col_index * CHAN_COL - owner * row_width
    windows = white.shape[2] * lax.axis_size("col")
    whole = lax.all_gather(white, "col", axis=2, tiled=True)
    own_part = lax.dynamic_slice_in_dim(whole, offset, CHAN_COL, 3)
    partner = spread(own_part, "row", owner)
    total = cross_block(whole, partner)
    return (total * (1.0 / math.sqrt(windows))).astype(jnp.bfloat16)


def solution(mesh):
    in_specs = (P("col", None, None, "row"), P(), P("col"))
    out_specs = P(None, None, "row", "col")
    return jax.shard_map(
        per_device, mesh=mesh, in_specs=in_specs, out_specs=out_specs, check_vma=False
    )
```

profile of v0, /device:TPU:1, one launch (start us, length us, event | category | flops | bytes accessed | tf_op | source)
XLA Modules:
  0.0 504.6 jit_solution(15202669938166275939)
XLA Ops:
  6.5 0.0 all-gather.2.cloned.1.call-start
  6.5 0.7 convert_element_type.16
  7.2 3.1 multiply_reduce_fusion
  10.3 0.1 rsqrt_multiply_fusion
  10.3 3.8 fusion.8
  14.1 0.0 all-gather.2.cloned.1.call-update
  14.2 0.0 all-reduce.2.cloned.1.call-start
  14.2 146.3 %all-gather.2.cloned.1.call-done = bf16[24,2,512,512]{3,0,1,2:T(8,128)(2,1)} async-done(((bf16[24,2,16,512]{3,0,1,2:T(8,128)(2,1)}), bf16[24,2,512,512]{3,0,1,2:T(8,128)(2,1)}) %all-gather.2.cloned.1.call-update) | async-done | bytes 25165840 | tf_op jit(solution)/shard_map/all_gather | solution.py:45
  160.5 24.5 %copy.13 = bf16[24,2,512,512]{3,2,1,0:T(8,128)(2,1)} copy(bf16[24,2,512,512]{3,0,1,2:T(8,128)(2,1)} %all-gather.2.cloned.1.call-done) | data formatting | bytes 50331648 | tf_op jit(solution)/shard_map/all_gather | solution.py:45
  185.0 7.5 %dynamic-slice_select_fusion = bf16[24,2,512,128]{3,2,1,0:T(8,128)(2,1)} fusion(bf16[24,2,512,512]{3,2,1,0:T(8,128)(2,1)} %copy.13, s32[]{:T(128)S(6)} %select_n.18, pred[]{:T(512)S(6)} %eq.19), kind=kLoop, calls=%fused_computation.8 | loop fusion | flops 3145728 | bytes 12582917 | tf_op jit(solution)/shard_map/jit(_where)/select_n | solution.py:12
  192.5 0.0 all-reduce.2.cloned.1.call-update
  192.5 17.2 %fusion.13 = (bf16[24,1,512,512]{3,0,1,2:T(8,128)(2,1)}, bf16[24,1,512,512]{3,0,1,2:T(8,128)(2,1)}) fusion(bf16[24,2,512,512]{3,0,1,2:T(8,128)(2,1)} %all-gather.2.cloned.1.call-done), kind=kLoop, calls=%fused_computation.18 | loop fusion | bytes 50331648 | tf_op jit(solution)/shard_map/slice | solution.py:30
  209.7 16.6 %copy.21 = bf16[24,1,512,512]{2,3,0,1:T(8,128)(2,1)} copy(bf16[24,1,512,512]{3,0,1,2:T(8,128)(2,1)} %get-tuple-element.5) | data formatting | bytes 25165824
  226.3 16.7 %copy.22 = bf16[24,1,512,512]{2,3,0,1:T(8,128)(2,1)} copy(bf16[24,1,512,512]{3,0,1,2:T(8,128)(2,1)} %get-tuple-element.6) | data formatting | bytes 25165824
  243.1 10.4 %negate_bitcast_fusion = bf16[24,512,512]{1,2,0:T(8,128)(2,1)} fusion(bf16[24,1,512,512]{2,3,0,1:T(8,128)(2,1)} %copy.22), kind=kLoop, calls=%fused_computation.6 | loop fusion | flops 6291456 | bytes 25165824 | tf_op jit(solution)/shard_map/neg | solution.py:30
  253.5 207.1 %all-reduce.2.cloned.1.call-done = bf16[24,1024,128]{2,1,0:T(8,128)(2,1)} async-done(((bf16[24,1024,128]{2,1,0:T(8,128)(2,1)}), bf16[24,1024,128]{2,1,0:T(8,128)(2,1)}) %all-reduce.2.cloned.1.call-update) | async-done | bytes 6291472 | tf_op jit(solution)/shard_map/psum | solution.py:13
  460.6 13.5 %convolution_bitcast_fusion = f32[24,1,512,128]{3,2,0,1:T(8,128)S(1)} fusion(bf16[24,1024,512]{2,1,0:T(8,128)(2,1)} %bitcast.20, bf16[24,1024,128]{2,1,0:T(8,128)(2,1)} %all-reduce.2.cloned.1.call-done), kind=kOutput, calls=%fused_computation.10 | convolution fusion | flops 3221225472 | bytes 37748736 | tf_op jit(solution)/shard_map/dot_general | solution.py:33
  474.0 16.3 %fusion.5 = f32[24,1,512,128]{3,2,0,1:T(8,128)} fusion(bf16[24,1024,128]{2,1,0:T(8,128)(2,1)} %all-reduce.2.cloned.1.call-done, bf16[24,512,512]{1,2,0:T(8,128)(2,1)} %negate_bitcast_fusion, bf16[24,512,512]{1,2,0:T(8,128)(2,1)} %bitcast.22), kind=kOutput, calls=%fused_computation.9 | convolution fusion | flops 3271557120 | bytes 37748736 | tf_op jit(solution)/shard_map/dot_general | solution.py:34
  490.3 4.3 fusion.4
  494.7 3.1 copy.18
Async XLA Ops:
  6.5 154.0 %all-gather.2.cloned.1.call-start = ((), (), s32[]{:S(2)}) async-start(), calls=%async_computation | async-start | bytes 25952256 | tf_op jit(solution)/shard_map/all_gather | solution.py:45
  14.2 446.4 %all-reduce.2.cloned.1.call-start = ((), (), s32[]{:S(2)}) async-start(), calls=%async_computation.1 | async-start | bytes 12582912 | tf_op jit(solution)/shard_map/psum | solution.py:13
Sparse Core Ops, SparseCore 0:
  14.3 146.1 all-gather.1
  192.7 267.8 all-reduce.1
where the time goes:
time: 506 us; the launch traced here: 505 us
  waiting for transfers between devices  353 us (70%)
  local copies, waits for them, and re-layouts  78.1 us (15%)
  matrix products  33.5 us (7%)
  other arithmetic  26 us (5%)
  between operations  13.4 us (3%)
    psum x1, waiting for transfers between devices, spread(): return lax.psum(block, axis)  207 us
    all_gather x1, waiting for transfers between devices, per_device(): whole = lax.all_gather(white, 'col', axis=2, tiled=True)  146 us
    unnamed x2, local copies, waits for them, and re-layouts  33.4 us
    all_gather x1, local copies, waits for them, and re-layouts, per_device(): whole = lax.all_gather(white, 'col', axis=2, tiled=True)  24.5 us
    slice x1, local copies, waits for them, and re-layouts, cross_block(): turned = jnp.concatenate([left_block[:, 1], -left_block[:, 0]], 1)  17.2 us
    dot_general x1, matrix products, cross_block(): lax.dot_general(turned, right, dims, preferred_element_type=jnp.float32)  16.3 us
    dot_general x1, matrix products, cross_block(): lax.dot_general(left, right, dims, preferred_element_type=jnp.float32)  13.5 us
    neg x1, other arithmetic, cross_block(): turned = jnp.concatenate([left_block[:, 1], -left_block[:, 0]], 1)  10.4 us
  transfers between devices with their start and end apart: 2, of which 2 were waited for; matrix products, arithmetic and copies ran while one was open for 12% of the time, Pallas kernels for 0%

commit v1 on v0

v1 whole, which is shorter than its diff:
```python
import functools
import math

import jax
import jax.numpy as jnp
from jax import lax
from jax.experimental import pallas as pl
from jax.experimental.pallas import tpu as pltpu
from jax.sharding import PartitionSpec as P

MESH = pl.DeviceIdType.MESH
NX, NY, NZ = 4, 4, 8
BPC = 6
CB = 128


def whiten_kernel(bins_ref, mask_ref, s_ref, o_ref, tmp):
    windows, parts, band, width = s_ref.shape
    nb = bins_ref.shape[0]
    rows = lax.broadcasted_iota(jnp.int32, (parts * nb, parts * band), 0)
    cols = lax.broadcasted_iota(jnp.int32, (parts * nb, parts * band), 1)
    hot = jnp.zeros((parts * nb, parts * band), jnp.float32)
    for f in range(nb):
        for p in range(parts):
            hit = (rows == p * nb + f) & (cols == p * band + bins_ref[f])
            hot = jnp.where(hit, 1.0, hot)
    hot = hot.astype(jnp.bfloat16)
    for w in range(windows):
        block = s_ref[w].reshape(parts * band, width)
        raw = block.astype(jnp.float32)
        power = jnp.sum(raw * raw, axis=0, keepdims=True) * (1.0 / (parts * band))
        factor = mask_ref[w].astype(jnp.float32) / jnp.sqrt(power + 1e-06)
        picked = jnp.dot(hot, block, preferred_element_type=jnp.float32) * factor
        tmp[pl.ds(w, parts * nb, stride=windows), :] = picked
    white = tmp[...].reshape(parts, nb, windows, width).astype(jnp.bfloat16)
    for p in range(parts):
        o_ref[:, p] = white[p]


def whiten(spectra, kept_bins, keep_mask):
    windows, parts, band, width = spectra.shape
    nb = kept_bins.shape[0]
    lanes = 128
    return pl.pallas_call(
        whiten_kernel,
        grid=(width // lanes,),
        out_shape=jax.ShapeDtypeStruct((nb, parts, windows, width), jnp.bfloat16),
        in_specs=[
            pl.BlockSpec(memory_space=pltpu.SMEM),
            pl.BlockSpec(memory_space=pltpu.SMEM),
            pl.BlockSpec((windows, parts, band, lanes), lambda i: (0, 0, 0, i)),
        ],
        out_specs=pl.BlockSpec((nb, parts, windows, lanes), lambda i: (0, 0, 0, i)),
        scratch_shapes=[pltpu.VMEM((parts * nb * windows, lanes), jnp.float32)],
        compiler_params=pltpu.CompilerParams(vmem_limit_bytes=32 * 2**20),
        name="whiten",
    )(kept_bins, keep_mask, spectra)


def stack_kernel(
    white, out, R, C, O,
    s1_send, s1_recv, zp_send, zp_recv, zm_send, zm_recv,
    c_send, c_recv, b_send, b_recv, o_send, o_recv,
):
    row, col = lax.axis_index("row"), lax.axis_index("col")
    y, xh = row // 2, row % 2
    xl, z, c = col // 16, (col // 2) % 8, col % 2
    x = xh * 2 + xl
    slot = xl * 2 + c

    def at(x_, y_, z_, c_):
        return ((y_ % NY) * 2 + x_ // 2, (x_ % 2) * 16 + (z_ % NZ) * 2 + c_)

    primary = c == (z % 4) // 2
    source = primary & (y % 2 == z // 4)
    xd_own = y // 2
    ch_off = pl.multiple_of((z % 2) * 2 * CB, 2 * CB)

    barrier = pltpu.get_barrier_semaphore()
    others = [at((x + dx) % NX, y, z, (c + dc) % 2) for dx in range(NX) for dc in range(2) if dx or dc]
    others += [at(x, y, z + 1, c), at(x, y, z + NZ - 1, c)]
    others += [at(x, y + d, z, c) for d in (1, 2, 3)]
    for who in others:
        pl.semaphore_signal(barrier, inc=1, device_id=who, device_id_type=MESH)
    pl.semaphore_wait(barrier, len(others))

    def remote(src, dst, ssem, rsem, who):
        return pltpu.make_async_remote_copy(
            src_ref=src, dst_ref=dst, send_sem=ssem, recv_sem=rsem, device_id=who, device_id_type=MESH
        )

    def s1_copy(j, xt):
        return remote(
            white.at[xt, j], R.at[j, :, 0, pl.ds(pl.multiple_of(slot * 16, 16), 16), :],
            s1_send.at[j, xt], s1_recv.at[j, slot], at(xt, y, z, xh),
        )

    def s1_start(j):
        for d in range(NX):
            xt = (x + d) % NX
            self_ = (xt == x) & (xh == c)

            @pl.when(self_)
            def _():
                pltpu.make_async_copy(
                    white.at[xt, j], R.at[j, :, 0, pl.ds(pl.multiple_of(slot * 16, 16), 16), :],
                    s1_recv.at[j, slot],
                ).start()

            @pl.when(jnp.logical_not(self_))
            def _():
                s1_copy(j, xt).start()

    def s1_wait(j):
        for s in range(4):
            dst = R.at[j, :, 0, pl.ds(s * 16, 16), :]
            pltpu.make_async_copy(dst, dst, s1_recv.at[j, s]).wait()

    def zp_copy(j, t):
        who = at(x, y, z + 1, c)
        if t == 3:
            src, dst = R.at[j, 0, 5], R.at[j, 0, 7]
        else:
            src, dst = R.at[j, :, max(2 * t - 1, 0)], R.at[j, :, 2 * t + 1]
        return remote(src, dst, zp_send.at[j, t], zp_recv.at[j, t], who)

    def zm_copy(j, t):
        who = at(x, y, z + NZ - 1, c)
        if t == 3:
            src, dst = R.at[j, 1, 6], R.at[j, 1, 7]
        else:
            src, dst = R.at[j, :, 2 * t], R.at[j, :, 2 * t + 2]
        return remote(src, dst, zm_send.at[j, t], zm_recv.at[j, t], who)

    def span(t):
        return pl.ds(0, 1) if t == 0 else pl.ds(7, 1) if t == 4 else pl.ds(2 * t - 1, 2)

    def c_views(j, t, xd):
        src = R.at[j, :, span(t), :, pl.ds(ch_off, 2 * CB)]
        dst = C.at[j, :, span(t), :, pl.ds(pl.multiple_of(xd * 2 * CB, 2 * CB), 2 * CB)]
        return src, dst

    def c_copy(j, t, d):
        src, dst = c_views(j, t, xd_own)
        return remote(src, dst, c_send.at[j, t, d - 1], c_recv.at[j, t, xd_own], at(x, y + d, z, c))

    def c_start(j, t):
        @pl.when(source)
        def _():
            for d in (2, 1, 3):
                c_copy(j, t, d).start()
            src, dst = c_views(j, t, xd_own)
            pltpu.make_async_copy(src, dst, c_recv.at[j, t, xd_own]).start()

    def b_copy(j, t):
        view = C.at[j, :, span(t)]
        return remote(view, view, b_send.at[j, t], b_recv.at[j, t], at(x, y, z, 1 - c))

    def c_forward(j, t):
        @pl.when(primary)
        def _():
            for xd in range(2):
                _src, dst = c_views(j, t, xd)
                pltpu.make_async_copy(dst, dst, c_recv.at[j, t, xd]).wait()
            b_copy(j, t).start()

    def c_arrived(j):
        @pl.when(jnp.logical_not(primary))
        def _():
            for t in range(5):
                b_copy(j, t).wait_recv()

    def hop(j, t):
        if t == 0:
            s1_wait(j)
        else:
            zp_copy(j, t - 1).wait_recv()
            zm_copy(j, t - 1).wait_recv()
        if t < 4:
            zp_copy(j, t).start()
            zm_copy(j, t).start()
        c_start(j, t)

    scale = 1.0 / math.sqrt(512)
    dims = (((0,), (0,)), ((), ()))

    def product(j, xd):
        depth = R.shape[2] * R.shape[3]
        cols = pl.ds(xd * 2 * CB, 2 * CB)
        r0 = C[j, 0, :, :, cols].reshape(depth, 2 * CB)
        r1 = C[j, 1, :, :, cols].reshape(depth, 2 * CB)
        for m in range(2):
            rows = pl.ds(m * 256, 256)
            l0 = R[j, 0, :, :, rows].reshape(depth, 256)
            l1 = R[j, 1, :, :, rows].reshape(depth, 256)
            dot = functools.partial(lax.dot_general, dimension_numbers=dims, preferred_element_type=jnp.float32)
            re = ((dot(l0, r0) + dot(l1, r1)) * scale).astype(jnp.bfloat16)
            im = ((dot(l1, r0) - dot(l0, r1)) * scale).astype(jnp.bfloat16)
            for k in range(2):
                O[j, xd, k, 0, rows, :] = re[:, k * CB:(k + 1) * CB]
                O[j, xd, k, 1, rows, :] = im[:, k * CB:(k + 1) * CB]

    def o_copy(j, xd, k):
        return remote(
            O.at[j, xd, k], out.at[x, j], o_send.at[j, xd * 2 + k], o_recv.at[j, x], at(2 * c + xd, y, z, k)
        )

    def is_self(xd, k):
        return (2 * c + xd == x) & (k == c)

    def o_start(j, xd):
        for k in range(2):
            @pl.when(is_self(xd, k))
            def _():
                pltpu.make_async_copy(O.at[j, xd, k], out.at[x, j], o_recv.at[j, x]).start()

            @pl.when(jnp.logical_not(is_self(xd, k)))
            def _():
                o_copy(j, xd, k).start()

    def s1_all(j, carry):
        s1_start(j)
        return carry

    lax.fori_loop(0, BPC, s1_all, 0)

    def step(i, carry):
        def on(j, f):
            @pl.when((j >= 0) & (j < BPC))
            def _():
                f(j)

        def first(j):
            hop(j, 4)
            c_forward(j, 3)

        def second(j):
            hop(j, 2)
            c_forward(j, 1)

        on(i - 2, first)
        on(i - 1, second)
        on(i, lambda j: hop(j, 0))

        def third(j):
            c_forward(j, 4)
            c_arrived(j)
            product(j, 0)
            o_start(j, 0)

        on(i - 2, third)

        def fourth(j):
            hop(j, 3)
            c_forward(j, 2)

        on(i - 1, fourth)

        def fifth(j):
            hop(j, 1)
            c_forward(j, 0)

        on(i, fifth)

        def sixth(j):
            product(j, 1)
            o_start(j, 1)

        on(i - 2, sixth)
        return carry

    lax.fori_loop(0, BPC + 2, step, 0)

    def drain(j, carry):
        for xt in range(NX):
            @pl.when(jnp.logical_not((xt == x) & (xh == c)))
            def _():
                s1_copy(j, xt).wait_send()
        for t in range(4):
            zp_copy(j, t).wait_send()
            zm_copy(j, t).wait_send()

        @pl.when(source)
        def _():
            for t in range(5):
                for d in (1, 2, 3):
                    c_copy(j, t, d).wait_send()

        @pl.when(primary)
        def _():
            for t in range(5):
                b_copy(j, t).wait_send()
        for xd in range(2):
            for k in range(2):
                @pl.when(jnp.logical_not(is_self(xd, k)))
                def _():
                    o_copy(j, xd, k).wait_send()
        for xs in range(NX):
            dst = out.at[xs, j]
            pltpu.make_async_copy(dst, dst, o_recv.at[j, xs]).wait()
        return carry

    lax.fori_loop(0, BPC, drain, 0)


def stack(white):
    sems = [(BPC, 4)] * 6 + [(BPC, 5, 3), (BPC, 5, 2), (BPC, 5), (BPC, 5), (BPC, 4), (BPC, 4)]
    width = white.shape[-1]
    return pl.pallas_call(
        stack_kernel,
        out_shape=jax.ShapeDtypeStruct((NX, BPC, 2, width, CB), jnp.bfloat16),
        in_specs=[pl.BlockSpec(memory_space=pl.ANY)],
        out_specs=pl.BlockSpec(memory_space=pl.ANY),
        scratch_shapes=[
            pltpu.VMEM((BPC, 2, NZ, 64, width), jnp.bfloat16),
            pltpu.VMEM((BPC, 2, NZ, 64, 4 * CB), jnp.bfloat16),
            pltpu.VMEM((BPC, 2, 2, 2, width, CB), jnp.bfloat16),
        ] + [pltpu.SemaphoreType.DMA(s) for s in sems],
        compiler_params=pltpu.CompilerParams(
            collective_id=0, has_side_effects=True, vmem_limit_bytes=48 * 2**20
        ),
        cost_estimate=pl.CostEstimate(flops=6_442_450_944, bytes_accessed=16 * 2**20, transcendentals=0),
        name="stack",
    )(white)


def per_device(spectra, kept_bins, keep_mask):
    white = whiten(spectra, kept_bins, keep_mask)
    nb, parts, windows, width = white.shape
    tiles = stack(white.reshape(NX, BPC, parts, windows, width))
    return tiles.reshape(nb, parts, width, CB)


def solution(mesh):
    in_specs = (P("col", None, None, "row"), P(), P("col"))
    out_specs = P(None, None, "row", "col")
    return jax.shard_map(
        per_device, mesh=mesh, in_specs=in_specs, out_specs=out_specs, check_vma=False
    )
```

time: 506 us -> 136 us (0.27)
  waiting for transfers between devices: 353 us -> 0 us
  Pallas kernels: 0 us -> 125 us
  local copies, waits for them, and re-layouts: 78.1 us -> 9.69 us
  matrix products: 33.5 us -> 0 us
  other arithmetic: 26 us -> 0 us
  between operations: 13.4 us -> 0.02 us
    psum x1 -> x0, waiting for transfers between devices: 207 us -> none  [spread(): return lax.psum(block, axis)]
    all_gather x1 -> x0, waiting for transfers between devices: 146 us -> none  [per_device(): whole = lax.all_gather(white, 'col', axis=2, tiled=True)]
    pallas_call x0 -> x2, Pallas kernels: none -> 125 us  [the longest x1 121 us: stack(): pl.pallas_call(stack_kernel, out_shape=jax.ShapeDtypeStruct((NX, BPC, 2,...]
    dot_general x3 -> x0, matrix products: 33.5 us -> none  [the longest x1 16.3 us: cross_block(): lax.dot_general(turned, right, dims, preferred_element_type=jnp.float32)]
    all_gather x1 -> x0, local copies, waits for them, and re-layouts: 24.5 us -> none  [per_device(): whole = lax.all_gather(white, 'col', axis=2, tiled=True)]
    unnamed x2 -> x7, local copies, waits for them, and re-layouts: 33.4 us -> 9.69 us
    slice x1 -> x0, local copies, waits for them, and re-layouts: 17.2 us -> none  [cross_block(): turned = jnp.concatenate([left_block[:, 1], -left_block[:, 0]], 1)]
    neg x1 -> x0, other arithmetic: 10.4 us -> none  [cross_block(): turned = jnp.concatenate([left_block[:, 1], -left_block[:, 0]], 1)]
  transfers between devices with their start and end apart: 2 -> 0, of which waited for: 2 -> 0; matrix products, arithmetic and copies ran while one was open for 12% -> 0% of each run, Pallas kernels for 0% -> 0%
where the time goes in v1:
time: 136 us; the launch traced here: 135 us
  Pallas kernels  125 us (92%)
  local copies, waits for them, and re-layouts  9.69 us (7%)
    pallas_call x1, Pallas kernels, stack(): pl.pallas_call(stack_kernel, out_shape=jax.ShapeDtypeStruct((NX, BPC, 2,...  121 us
    unnamed x7, local copies, waits for them, and re-layouts  9.69 us
    pallas_call x1, Pallas kernels, whiten(): pl.pallas_call(whiten_kernel, grid=(width // lanes,), out_shape=jax.Shape...  3.68 us

profile of v1, /device:TPU:1, one launch (start us, length us, event | category | flops | bytes accessed | tf_op | source)
XLA Modules:
  0.0 134.8 jit_solution(1688735084450029190)
XLA Ops:
  0.0 0.0 copy-start
  0.0 2.2 %copy-done = bf16[16,2,128,512]{3,2,1,0:T(8,128)(2,1)S(1)} copy-done((bf16[16,2,128,512]{3,2,1,0:T(8,128)(2,1)S(1)}, bf16[16,2,128,512]{3,2,1,0:T(8,128)(2,1)}, u32[]{:S(2)}) %copy-start) | copy-done | bytes 4194328
  2.2 0.0 copy-start.1
  2.2 0.7 copy-done.1
  2.8 0.0 copy-start.2
  2.8 0.7 copy-done.2
  3.5 3.7 %whiten.1 = bf16[24,2,16,512]{3,2,1,0:T(8,128)(2,1)S(1)} custom-call(s32[24]{0:T(128)S(1)} %copy-done.1, s32[16]{0:T(128)S(1)} %copy-done.2, bf16[16,2,128,512]{3,2,1,0:T(8,128)(2,1)S(1)} %copy-done), custom_call_target="tpu_custom_call" | custom-call | tf_op jit(solution)/shard_map/whiten/pallas_call | solution.py:44
  7.2 121.5 %stack.1 = bf16[4,6,2,512,128]{4,3,2,1,0:T(8,128)(2,1)} custom-call(bf16[4,6,2,16,512]{4,3,2,1,0:T(8,128)(2,1)S(1)} %bitcast.2), custom_call_target="tpu_custom_call" | custom-call | flops 6442450944 | bytes 16777216 | tf_op jit(solution)/shard_map/stack/pallas_call | solution.py:309
  128.7 6.2 %copy.5 = bf16[24,2,512,128]{3,2,1,0:T(8,128)(2,1)} copy(bf16[24,2,512,128]{3,2,1,0:T(8,128)(2,1)} %bitcast.3) | data formatting | bytes 12582912
Async XLA Ops:
  0.0 2.2 %copy-start = (bf16[16,2,128,512]{3,2,1,0:T(8,128)(2,1)S(1)}, bf16[16,2,128,512]{3,2,1,0:T(8,128)(2,1)}, u32[]{:S(2)}) copy-start(bf16[16,2,128,512]{3,2,1,0:T(8,128)(2,1)} %s_ref.1) | copy-start | bytes 12582916
  2.2 0.7 copy-start.1
  2.8 0.7 copy-start.2

commit v2 on v0

v2 whole, which is shorter than its diff:
```python
import functools
import math

import jax
import jax.numpy as jnp
from jax import lax
from jax.experimental import pallas as pl
from jax.experimental.pallas import tpu as pltpu
from jax.sharding import PartitionSpec as P

MESH = pl.DeviceIdType.MESH
NX, NY, NZ = 4, 4, 8
BPC = 6
CB = 128
NH = 1


def stack_kernel(
    bins_ref, mask_ref, spectra, out, raw, picked, white, R, C, O,
    in_sem, s1_send, s1_recv, z_send, z_recv, c_send, c_recv, b_send, b_recv, o_send, o_recv,
):
    row, col = lax.axis_index("row"), lax.axis_index("col")
    y, xh = row // 2, row % 2
    xl, z, c = col // 16, (col // 2) % 8, col % 2
    x = xh * 2 + xl
    slot = xl * 2 + c

    def at(x_, y_, z_, c_):
        return ((y_ % NY) * 2 + x_ // 2, (x_ % 2) * 16 + (z_ % NZ) * 2 + c_)

    holder = (z % 4) // 2
    source = (c == holder) & (y % 2 == z // 4)
    to_core = y // 2
    ch_off = pl.multiple_of((z % 2) * 2 * CB, 2 * CB)
    y_from = 2 * c + z // 4

    barrier = pltpu.get_barrier_semaphore()

    def greet(who):
        pl.semaphore_signal(barrier, inc=1, device_id=who, device_id_type=MESH)

    ring = [at((x + dx) % NX, y, z, (c + dc) % 2) for dx in range(NX) for dc in range(2) if dx or dc]
    ring += [at(x, y, z + 1, c), at(x, y, z + NZ - 1, c)]
    for who in ring:
        greet(who)

    @pl.when(y_from != y)
    def _():
        greet(at(x, y_from, z, holder))

    windows, parts, band, width = raw.shape
    nb = bins_ref.shape[0]

    def in_copy(i):
        part = pl.ds(4 * i, 4)
        return pltpu.make_async_copy(spectra.at[part], raw.at[part], in_sem.at[i])

    for i in range(windows // 4):
        in_copy(i).start()
    rows = lax.broadcasted_iota(jnp.int32, (parts * nb, parts * band), 0)
    cols = lax.broadcasted_iota(jnp.int32, (parts * nb, parts * band), 1)
    place = jnp.full((parts * nb, parts * band), -1, jnp.int32)
    for f in range(nb):
        for p in range(parts):
            place = jnp.where(rows == p * nb + f, bins_ref[f] + p * band, place)
    hot = jnp.where(cols == place, 1.0, 0.0).astype(jnp.bfloat16)

    def whiten(i, carry):
        in_copy(i).wait()
        for k in range(4):
            w = 4 * i + k
            block = raw[w].reshape(parts * band, width)
            wide = block.astype(jnp.float32)
            power = jnp.sum(wide * wide, axis=0, keepdims=True) * (1.0 / (parts * band))
            factor = mask_ref[w].astype(jnp.float32) / jnp.sqrt(power + 1e-06)
            kept = jnp.dot(hot, block, preferred_element_type=jnp.float32) * factor
            for l in range(width // 128):
                picked[l, pl.ds(w, parts * nb, stride=windows), :] = kept[:, l * 128:(l + 1) * 128]
        return carry

    lax.fori_loop(0, windows // 4, whiten, 0)
    pl.semaphore_wait(barrier, len(ring) + jnp.where(source, NY - 1, 0))

    def remote(src, dst, ssem, rsem, who):
        return pltpu.make_async_remote_copy(
            src_ref=src, dst_ref=dst, send_sem=ssem, recv_sem=rsem, device_id=who, device_id_type=MESH
        )

    def s1_copy(j, xt):
        return remote(
            white.at[xt, j], R.at[xh, j, :, 0, pl.ds(pl.multiple_of(slot * 16, 16), 16), :],
            s1_send.at[xt], s1_recv.at[j], at(xt, y, z, xh),
        )

    def s1_start(j):
        for d in range(NX):
            xt = (x + d) % NX
            self_ = (xt == x) & (xh == c)

            @pl.when(self_)
            def _():
                pltpu.make_async_copy(
                    white.at[xt, j], R.at[xh, j, :, 0, pl.ds(pl.multiple_of(slot * 16, 16), 16), :],
                    s1_recv.at[j],
                ).start()

            @pl.when(jnp.logical_not(self_))
            def _():
                s1_copy(j, xt).start()

    def s1_wait(j):
        dst = R.at[c, j, :, 0]
        pltpu.make_async_copy(dst, dst, s1_recv.at[j]).wait()

    def z_copy(j, t, p, h, way):
        rows = pl.ds(h * (64 // NH), 64 // NH)
        if way == 0:
            here, there, who = max(2 * t - 1, 0), 2 * t + 1, at(x, y, z + 1, c)
        else:
            here, there, who = 2 * t, 7 if t == 3 else 2 * t + 2, at(x, y, z + NZ - 1, c)
        return remote(
            R.at[c, j, p, here, rows], R.at[c, j, p, there, rows],
            z_send.at[way], z_recv.at[j % 2, t, p, h, way], who,
        )

    def z_goes(t, p, way):
        return 0 <= t < 3 or (t == 3 and way == p)

    def span(t):
        return {1: pl.ds(0, 3), 2: pl.ds(3, 2), 3: pl.ds(5, 2), 4: pl.ds(7, 1)}[t]

    def b_copy(j, view):
        view = R.at[c, j, :, view]
        return remote(view, view, b_send, b_recv.at[j], at(x, y, z, 1 - c))

    def c_copy(j, view, d):
        src, dst = R.at[c, j, :, view, :, pl.ds(ch_off, 2 * CB)], C.at[j, :, view]
        return remote(src, dst, c_send.at[d], c_recv.at[j], at(x, y + d, z, to_core))

    def share(j, t):
        @pl.when(source)
        def _():
            for d in (2, 1, 3):
                c_copy(j, span(t), d).start()

            @pl.when(c == to_core)
            def _():
                pltpu.make_async_copy(
                    R.at[c, j, :, span(t), :, pl.ds(ch_off, 2 * CB)], C.at[j, :, span(t)], c_recv.at[j]
                ).start()

            @pl.when(c != to_core)
            def _():
                c_copy(j, span(t), 0).start()

        b_copy(j, span(t)).start()

    def shared(j):
        dst = R.at[1 - c, j]
        pltpu.make_async_copy(dst, dst, b_recv.at[j]).wait()
        pltpu.make_async_copy(C.at[j], C.at[j], c_recv.at[j]).wait()

    def hop(j, t):
        if t == 0:
            s1_wait(j)
        for p in range(parts):
            for h in range(NH):
                for way in range(2):
                    if z_goes(t - 1, p, way):
                        z_copy(j, t - 1, p, h, way).wait_recv()
                    if z_goes(t, p, way):
                        z_copy(j, t, p, h, way).start()
        if t > 0:
            share(j, t)

    scale = 1.0 / math.sqrt(512)
    dims = (((0,), (0,)), ((), ()))

    def product(j, xr, m):
        depth = R.shape[3] * R.shape[4]
        rows = pl.ds(m * 256, 256)
        r0, r1 = (C[j, p].reshape(depth, 2 * CB) for p in range(parts))
        l0, l1 = (R[xr, j, p, :, :, rows].reshape(depth, 256) for p in range(parts))
        dot = functools.partial(lax.dot_general, dimension_numbers=dims, preferred_element_type=jnp.float32)
        re = ((dot(l0, r0) + dot(l1, r1)) * scale).astype(jnp.bfloat16)
        im = ((dot(l1, r0) - dot(l0, r1)) * scale).astype(jnp.bfloat16)
        for k in range(2):
            O[j, xr, k, 0, rows, :] = re[:, k * CB:(k + 1) * CB]
            O[j, xr, k, 1, rows, :] = im[:, k * CB:(k + 1) * CB]
        o_start(j, xr, m)

    def o_copy(j, xr, k, m):
        rows = pl.ds(m * 256, 256)
        return remote(
            O.at[j, xr, k, :, rows], out.at[x, j, :, rows],
            o_send.at[xr * 2 + k], o_recv, at(2 * xr + c, y, z, k)
        )

    def is_self(xr, k):
        return (2 * xr + c == x) & (k == c)

    def o_start(j, xr, m):
        rows = pl.ds(m * 256, 256)
        for k in range(2):
            @pl.when(is_self(xr, k))
            def _():
                pltpu.make_async_copy(
                    O.at[j, xr, k, :, rows], out.at[x, j, :, rows], o_recv
                ).start()

            @pl.when(jnp.logical_not(is_self(xr, k)))
            def _():
                o_copy(j, xr, k, m).start()

    def s1_bin(j):
        for l in range(width // 128):
            for xt in range(NX):
                for p in range(parts):
                    start = pl.multiple_of((p * nb + xt * BPC + j) * windows, windows)
                    tile = picked[l, pl.ds(start, windows), :]
                    white[xt, j, p, :, l * 128:(l + 1) * 128] = tile.astype(jnp.bfloat16)
        s1_start(j)

    s1_bin(0)
    hop(0, 0)
    s1_bin(1)
    hop(0, 1)
    s1_bin(2)
    hop(0, 2)
    hop(1, 0)

    def step(i, carry):
        def on(j, *work):
            @pl.when((j >= 0) & (j < BPC))
            def _():
                for f, *args in work:
                    f(j, *args)

        on(i, (hop, 3))
        on(i - 1, (product, 0, 1))
        on(i + 1, (hop, 1))
        on(i - 1, (product, 1, 0))
        on(i, (hop, 4))
        on(i - 1, (product, 1, 1))
        on(i + 2, (hop, 0))
        on(i + 1, (hop, 2))
        on(i + 3, (s1_bin,))
        on(i, (shared,), (product, 0, 0))
        return carry

    lax.fori_loop(0, BPC + 1, step, 0)

    def sent(view, sem):
        remote(view, view, sem, o_recv, at(x, y, z, 1 - c)).wait_send()

    for xt in range(NX):
        @pl.when(jnp.logical_not((xt == x) & (xh == c)))
        def _():
            sent(white.at[xt], s1_send.at[xt])
    for way in range(2):
        sent(R.at[c, :, 0, pl.ds(0, 7)], z_send.at[way])
    sent(R.at[c], b_send)

    @pl.when(source)
    def _():
        for d in range(1, 4):
            sent(C, c_send.at[d])

        @pl.when(c != to_core)
        def _():
            sent(C, c_send.at[0])

    for xr in range(2):
        for k in range(2):
            @pl.when(jnp.logical_not(is_self(xr, k)))
            def _():
                sent(O.at[:, xr, k], o_send.at[xr * 2 + k])
    pltpu.make_async_copy(out, out, o_recv).wait()


def per_device(spectra, kept_bins, keep_mask):
    windows, parts, band, width = spectra.shape
    nb = kept_bins.shape[0]
    sems = [(windows // 4,), (NX,), (BPC,), (2,), (2, 4, 2, NH, 2), (NY,), (BPC,), (), (BPC,), (4,), ()]
    tiles = pl.pallas_call(
        stack_kernel,
        out_shape=pltpu.VMEM((NX, BPC, parts, width, CB), jnp.bfloat16),
        in_specs=[
            pl.BlockSpec(memory_space=pltpu.SMEM),
            pl.BlockSpec(memory_space=pltpu.SMEM),
            pl.BlockSpec(memory_space=pltpu.HBM),
        ],
        out_specs=pl.BlockSpec(memory_space=pl.ANY),
        scratch_shapes=[
            pltpu.VMEM((windows, parts, band, width), jnp.bfloat16),
            pltpu.VMEM((width // 128, parts * nb * windows, 128), jnp.float32),
            pltpu.VMEM((NX, BPC, parts, windows, width), jnp.bfloat16),
            pltpu.VMEM((2, BPC, parts, NZ, 4 * windows, width), jnp.bfloat16),
            pltpu.VMEM((BPC, parts, NZ, 4 * windows, 2 * CB), jnp.bfloat16),
            pltpu.VMEM((BPC, 2, 2, parts, width, CB), jnp.bfloat16),
        ] + [pltpu.SemaphoreType.DMA(s) for s in sems],
        compiler_params=pltpu.CompilerParams(
            collective_id=0, has_side_effects=True, vmem_limit_bytes=54 * 2**20
        ),
        cost_estimate=pl.CostEstimate(flops=6_442_450_944, bytes_accessed=16 * 2**20, transcendentals=0),
        name="stack",
    )(kept_bins, keep_mask, spectra)
    return tiles.reshape(nb, parts, width, CB)


def solution(mesh):
    in_specs = (P("col", None, None, "row"), P(), P("col"))
    out_specs = P(None, None, "row", "col")
    return jax.shard_map(
        per_device, mesh=mesh, in_specs=in_specs, out_specs=out_specs, check_vma=False
    )
```

time: 506 us -> 115 us (0.23)
  waiting for transfers between devices: 353 us -> 0 us
  Pallas kernels: 0 us -> 112 us
  local copies, waits for them, and re-layouts: 78.1 us -> 2.71 us
  matrix products: 33.5 us -> 0 us
  other arithmetic: 26 us -> 0 us
  between operations: 13.4 us -> 0.01 us
    psum x1 -> x0, waiting for transfers between devices: 207 us -> none  [spread(): return lax.psum(block, axis)]
    all_gather x1 -> x0, waiting for transfers between devices: 146 us -> none  [per_device(): whole = lax.all_gather(white, 'col', axis=2, tiled=True)]
    pallas_call x0 -> x1, Pallas kernels: none -> 112 us  [per_device(): pl.pallas_call(stack_kernel, out_shape=pltpu.VMEM((NX, BPC, parts, width,...]
    dot_general x3 -> x0, matrix products: 33.5 us -> none  [the longest x1 16.3 us: cross_block(): lax.dot_general(turned, right, dims, preferred_element_type=jnp.float32)]
    unnamed x2 -> x1, local copies, waits for them, and re-layouts: 33.4 us -> 2.71 us
    all_gather x1 -> x0, local copies, waits for them, and re-layouts: 24.5 us -> none  [per_device(): whole = lax.all_gather(white, 'col', axis=2, tiled=True)]
    slice x1 -> x0, local copies, waits for them, and re-layouts: 17.2 us -> none  [cross_block(): turned = jnp.concatenate([left_block[:, 1], -left_block[:, 0]], 1)]
    neg x1 -> x0, other arithmetic: 10.4 us -> none  [cross_block(): turned = jnp.concatenate([left_block[:, 1], -left_block[:, 0]], 1)]
  transfers between devices with their start and end apart: 2 -> 0, of which waited for: 2 -> 0; matrix products, arithmetic and copies ran while one was open for 12% -> 0% of each run, Pallas kernels for 0% -> 0%
where the time goes in v2:
time: 115 us
  Pallas kernels  112 us (97%)
  local copies, waits for them, and re-layouts  2.71 us (2%)
    pallas_call x1, Pallas kernels, per_device(): pl.pallas_call(stack_kernel, out_shape=pltpu.VMEM((NX, BPC, parts, width,...  112 us
    unnamed x1, local copies, waits for them, and re-layouts  2.71 us

profile of v2, /device:TPU:1, one launch (start us, length us, event | category | flops | bytes accessed | tf_op | source)
XLA Modules:
  0.0 114.6 jit_solution(17156439896700558977)
XLA Ops:
  0.0 111.9 %stack.1 = bf16[4,6,2,512,128]{4,3,2,1,0:T(8,128)(2,1)S(1)} custom-call(s32[24]{0:T(128)} %bins_ref.1, s32[16]{0:T(128)} %mask_ref.1, bf16[16,2,128,512]{3,2,1,0:T(8,128)(2,1)} %spectra.1), custom_call_target="tpu_custom_call" | custom-call | flops 6442450944 | bytes 16777216 | tf_op jit(solution)/shard_map/stack/pallas_call | solution.py:285
  111.9 2.7 %copy.5 = bf16[24,2,512,128]{3,2,1,0:T(8,128)(2,1)} copy(bf16[24,2,512,128]{3,2,1,0:T(8,128)(2,1)S(1)} %bitcast.1) | data formatting | bytes 12582912

commit v3 on v2

--- a/solution.py
+++ b/solution.py
@@ -12,7 +12,7 @@
 NX, NY, NZ = 4, 4, 8
 BPC = 6
 CB = 128
-NH = 1
+NH = 2
 
 
 def stack_kernel(
@@ -31,7 +31,6 @@
     holder = (z % 4) // 2
     source = (c == holder) & (y % 2 == z // 4)
     to_core = y // 2
-    ch_off = pl.multiple_of((z % 2) * 2 * CB, 2 * CB)
     y_from = 2 * c + z // 4
 
     barrier = pltpu.get_barrier_semaphore()
@@ -88,8 +87,8 @@
 
     def s1_copy(j, xt):
         return remote(
-            white.at[xt, j], R.at[xh, j, :, 0, pl.ds(pl.multiple_of(slot * 16, 16), 16), :],
-            s1_send.at[xt], s1_recv.at[j], at(xt, y, z, xh),
+            white.at[xt, j], R.at[xh, j, :, 0, :, pl.ds(pl.multiple_of(slot * 16, 16), 16), :],
+            s1_send.at[xt], s1_recv.at[j, xl], at(xt, y, z, xh),
         )
 
     def s1_start(j):
@@ -100,17 +99,17 @@
             @pl.when(self_)
             def _():
                 pltpu.make_async_copy(
-                    white.at[xt, j], R.at[xh, j, :, 0, pl.ds(pl.multiple_of(slot * 16, 16), 16), :],
-                    s1_recv.at[j],
+                    white.at[xt, j], R.at[xh, j, :, 0, :, pl.ds(pl.multiple_of(slot * 16, 16), 16), :],
+                    s1_recv.at[j, xl],
                 ).start()
 
             @pl.when(jnp.logical_not(self_))
             def _():
                 s1_copy(j, xt).start()
 
-    def s1_wait(j):
-        dst = R.at[c, j, :, 0]
-        pltpu.make_async_copy(dst, dst, s1_recv.at[j]).wait()
+    def s1_wait(j, h):
+        dst = R.at[c, j, :, 0, :, pl.ds(h * 32, 32)]
+        pltpu.make_async_copy(dst, dst, s1_recv.at[j, h]).wait()
 
     def z_copy(j, t, p, h, way):
         rows = pl.ds(h * (64 // NH), 64 // NH)
@@ -119,7 +118,7 @@
         else:
             here, there, who = 2 * t, 7 if t == 3 else 2 * t + 2, at(x, y, z + NZ - 1, c)
         return remote(
-            R.at[c, j, p, here, rows], R.at[c, j, p, there, rows],
+            R.at[c, j, p, here, :, rows], R.at[c, j, p, there, :, rows],
             z_send.at[way], z_recv.at[j % 2, t, p, h, way], who,
         )
 
@@ -134,7 +133,7 @@
         return remote(view, view, b_send, b_recv.at[j], at(x, y, z, 1 - c))
 
     def c_copy(j, view, d):
-        src, dst = R.at[c, j, :, view, :, pl.ds(ch_off, 2 * CB)], C.at[j, :, view]
+        src, dst = R.at[c, j, :, view, z % 2], C.at[j, :, view]
         return remote(src, dst, c_send.at[d], c_recv.at[j], at(x, y + d, z, to_core))
 
     def share(j, t):
@@ -146,7 +145,7 @@
             @pl.when(c == to_core)
             def _():
                 pltpu.make_async_copy(
-                    R.at[c, j, :, span(t), :, pl.ds(ch_off, 2 * CB)], C.at[j, :, span(t)], c_recv.at[j]
+                    R.at[c, j, :, span(t), z % 2], C.at[j, :, span(t)], c_recv.at[j]
                 ).start()
 
             @pl.when(c != to_core)
@@ -161,10 +160,10 @@
         pltpu.make_async_copy(C.at[j], C.at[j], c_recv.at[j]).wait()
 
     def hop(j, t):
-        if t == 0:
-            s1_wait(j)
-        for p in range(parts):
-            for h in range(NH):
+        for h in range(NH):
+            if t == 0:
+                s1_wait(j, h)
+            for p in range(parts):
                 for way in range(2):
                     if z_goes(t - 1, p, way):
                         z_copy(j, t - 1, p, h, way).wait_recv()
@@ -177,10 +176,10 @@
     dims = (((0,), (0,)), ((), ()))
 
     def product(j, xr, m):
-        depth = R.shape[3] * R.shape[4]
+        depth = R.shape[3] * R.shape[5]
         rows = pl.ds(m * 256, 256)
         r0, r1 = (C[j, p].reshape(depth, 2 * CB) for p in range(parts))
-        l0, l1 = (R[xr, j, p, :, :, rows].reshape(depth, 256) for p in range(parts))
+        l0, l1 = (R[xr, j, p, :, m].reshape(depth, 256) for p in range(parts))
         dot = functools.partial(lax.dot_general, dimension_numbers=dims, preferred_element_type=jnp.float32)
         re = ((dot(l0, r0) + dot(l1, r1)) * scale).astype(jnp.bfloat16)
         im = ((dot(l1, r0) - dot(l0, r1)) * scale).astype(jnp.bfloat16)
@@ -218,14 +217,17 @@
                 for p in range(parts):
                     start = pl.multiple_of((p * nb + xt * BPC + j) * windows, windows)
                     tile = picked[l, pl.ds(start, windows), :]
-                    white[xt, j, p, :, l * 128:(l + 1) * 128] = tile.astype(jnp.bfloat16)
+                    white[xt, j, p, l // 2, :, l % 2 * 128:(l % 2 + 1) * 128] = tile.astype(jnp.bfloat16)
         s1_start(j)
 
     s1_bin(0)
     hop(0, 0)
     s1_bin(1)
+    s1_bin(2)
     hop(0, 1)
-    s1_bin(2)
+    s1_bin(3)
+    s1_bin(4)
+    s1_bin(5)
     hop(0, 2)
     hop(1, 0)
 
@@ -244,7 +246,6 @@
         on(i - 1, (product, 1, 1))
         on(i + 2, (hop, 0))
         on(i + 1, (hop, 2))
-        on(i + 3, (s1_bin,))
         on(i, (shared,), (product, 0, 0))
         return carry
 
@@ -281,7 +282,7 @@
 def per_device(spectra, kept_bins, keep_mask):
     windows, parts, band, width = spectra.shape
     nb = kept_bins.shape[0]
-    sems = [(windows // 4,), (NX,), (BPC,), (2,), (2, 4, 2, NH, 2), (NY,), (BPC,), (), (BPC,), (4,), ()]
+    sems = [(windows // 4,), (NX,), (BPC, NH), (2,), (2, 4, 2, NH, 2), (NY,), (BPC,), (), (BPC,), (4,), ()]
     tiles = pl.pallas_call(
         stack_kernel,
         out_shape=pltpu.VMEM((NX, BPC, parts, width, CB), jnp.bfloat16),
@@ -294,8 +295,8 @@
         scratch_shapes=[
             pltpu.VMEM((windows, parts, band, width), jnp.bfloat16),
             pltpu.VMEM((width // 128, parts * nb * windows, 128), jnp.float32),
-            pltpu.VMEM((NX, BPC, parts, windows, width), jnp.bfloat16),
-            pltpu.VMEM((2, BPC, parts, NZ, 4 * windows, width), jnp.bfloat16),
+            pltpu.VMEM((NX, BPC, parts, 2, windows, 2 * CB), jnp.bfloat16),
+            pltpu.VMEM((2, BPC, parts, NZ, 2, 4 * windows, 2 * CB), jnp.bfloat16),
             pltpu.VMEM((BPC, parts, NZ, 4 * windows, 2 * CB), jnp.bfloat16),
             pltpu.VMEM((BPC, 2, 2, parts, width, CB), jnp.bfloat16),
         ] + [pltpu.SemaphoreType.DMA(s) for s in sems],

time: 115 us -> 113 us (0.983)
  Pallas kernels: 112 us -> 110 us
    pallas_call x1, Pallas kernels: 112 us -> 110 us  [per_device(): pl.pallas_call(stack_kernel, out_shape=pltpu.VMEM((NX, BPC, parts, width,...]
where the time goes in v3:
time: 113 us
  Pallas kernels  110 us (97%)
  local copies, waits for them, and re-layouts  2.71 us (2%)
    pallas_call x1, Pallas kernels, per_device(): pl.pallas_call(stack_kernel, out_shape=pltpu.VMEM((NX, BPC, parts, width,...  110 us
    unnamed x1, local copies, waits for them, and re-layouts  2.71 us

profile of v3, /device:TPU:1, one launch (start us, length us, event | category | flops | bytes accessed | tf_op | source)
XLA Modules:
  0.0 113.1 jit_solution(15799383173685660693)
XLA Ops:
  0.0 110.4 %stack.1 = bf16[4,6,2,512,128]{4,3,2,1,0:T(8,128)(2,1)S(1)} custom-call(s32[24]{0:T(128)} %bins_ref.1, s32[16]{0:T(128)} %mask_ref.1, bf16[16,2,128,512]{3,2,1,0:T(8,128)(2,1)} %spectra.1), custom_call_target="tpu_custom_call" | custom-call | flops 6442450944 | bytes 16777216 | tf_op jit(solution)/shard_map/stack/pallas_call | solution.py:286
  110.4 2.7 %copy.5 = bf16[24,2,512,128]{3,2,1,0:T(8,128)(2,1)} copy(bf16[24,2,512,128]{3,2,1,0:T(8,128)(2,1)S(1)} %bitcast.1) | data formatting | bytes 12582912

commit v4 on v3

--- a/solution.py
+++ b/solution.py
@@ -126,7 +126,7 @@
         return 0 <= t < 3 or (t == 3 and way == p)
 
     def span(t):
-        return {1: pl.ds(0, 3), 2: pl.ds(3, 2), 3: pl.ds(5, 2), 4: pl.ds(7, 1)}[t]
+        return pl.ds(0, 1) if t == 0 else pl.ds(7, 1) if t == 4 else pl.ds(2 * t - 1, 2)
 
     def b_copy(j, view):
         view = R.at[c, j, :, view]
@@ -169,20 +169,22 @@
                         z_copy(j, t - 1, p, h, way).wait_recv()
                     if z_goes(t, p, way):
                         z_copy(j, t, p, h, way).start()
-        if t > 0:
-            share(j, t)
+        share(j, t)
 
     scale = 1.0 / math.sqrt(512)
     dims = (((0,), (0,)), ((), ()))
 
-    def product(j, xr, m):
+    def product(j, turn, m):
+        xr = jnp.where(turn == 0, 1 - x // 2, x // 2)
         depth = R.shape[3] * R.shape[5]
         rows = pl.ds(m * 256, 256)
         r0, r1 = (C[j, p].reshape(depth, 2 * CB) for p in range(parts))
         l0, l1 = (R[xr, j, p, :, m].reshape(depth, 256) for p in range(parts))
+        both = jnp.concatenate([r0, r1], 1)
         dot = functools.partial(lax.dot_general, dimension_numbers=dims, preferred_element_type=jnp.float32)
-        re = ((dot(l0, r0) + dot(l1, r1)) * scale).astype(jnp.bfloat16)
-        im = ((dot(l1, r0) - dot(l0, r1)) * scale).astype(jnp.bfloat16)
+        by0, by1 = dot(l0, both), dot(l1, both)
+        re = ((by0[:, :2 * CB] + by1[:, 2 * CB:]) * scale).astype(jnp.bfloat16)
+        im = ((by1[:, :2 * CB] - by0[:, 2 * CB:]) * scale).astype(jnp.bfloat16)
         for k in range(2):
             O[j, xr, k, 0, rows, :] = re[:, k * CB:(k + 1) * CB]
             O[j, xr, k, 1, rows, :] = im[:, k * CB:(k + 1) * CB]

time: 113 us -> 111 us (0.982); the launches traced: 113 us -> 110 us
  Pallas kernels: 110 us -> 107 us
    pallas_call x1, Pallas kernels: 110 us -> 107 us  [per_device(): pl.pallas_call(stack_kernel, out_shape=pltpu.VMEM((NX, BPC, parts, width,...]
where the time goes in v4:
time: 111 us; the launch traced here: 110 us
  Pallas kernels  107 us (96%)
  local copies, waits for them, and re-layouts  2.71 us (2%)
    pallas_call x1, Pallas kernels, per_device(): pl.pallas_call(stack_kernel, out_shape=pltpu.VMEM((NX, BPC, parts, width,...  107 us
    unnamed x1, local copies, waits for them, and re-layouts  2.71 us

profile of v4, /device:TPU:1, one launch (start us, length us, event | category | flops | bytes accessed | tf_op | source)
XLA Modules:
  0.0 109.9 jit_solution(9316747666221758859)
XLA Ops:
  0.0 107.2 %stack.1 = bf16[4,6,2,512,128]{4,3,2,1,0:T(8,128)(2,1)S(1)} custom-call(s32[24]{0:T(128)} %bins_ref.1, s32[16]{0:T(128)} %mask_ref.1, bf16[16,2,128,512]{3,2,1,0:T(8,128)(2,1)} %spectra.1), custom_call_target="tpu_custom_call" | custom-call | flops 6442450944 | bytes 16777216 | tf_op jit(solution)/shard_map/stack/pallas_call | solution.py:288
  107.2 2.7 %copy.5 = bf16[24,2,512,128]{3,2,1,0:T(8,128)(2,1)} copy(bf16[24,2,512,128]{3,2,1,0:T(8,128)(2,1)S(1)} %bitcast.1) | data formatting | bytes 12582912

commit v5 on v4

--- a/solution.py
+++ b/solution.py
@@ -246,8 +246,8 @@
         on(i - 1, (product, 1, 0))
         on(i, (hop, 4))
         on(i - 1, (product, 1, 1))
+        on(i + 1, (hop, 2))
         on(i + 2, (hop, 0))
-        on(i + 1, (hop, 2))
         on(i, (shared,), (product, 0, 0))
         return carry
 

time: 111 us -> 110 us (level)
  no operation moved by 1% of the time
where the time goes in v5:
time: 110 us
  Pallas kernels  107 us (97%)
  local copies, waits for them, and re-layouts  2.71 us (2%)
    pallas_call x1, Pallas kernels, per_device(): pl.pallas_call(stack_kernel, out_shape=pltpu.VMEM((NX, BPC, parts, width,...  107 us
    unnamed x1, local copies, waits for them, and re-layouts  2.71 us

profile of v5, /device:TPU:1, one launch (start us, length us, event | category | flops | bytes accessed | tf_op | source)
XLA Modules:
  0.0 109.7 jit_solution(9685040753432159516)
XLA Ops:
  0.0 107.0 %stack.1 = bf16[4,6,2,512,128]{4,3,2,1,0:T(8,128)(2,1)S(1)} custom-call(s32[24]{0:T(128)} %bins_ref.1, s32[16]{0:T(128)} %mask_ref.1, bf16[16,2,128,512]{3,2,1,0:T(8,128)(2,1)} %spectra.1), custom_call_target="tpu_custom_call" | custom-call | flops 6442450944 | bytes 16777216 | tf_op jit(solution)/shard_map/stack/pallas_call | solution.py:288
  107.0 2.7 %copy.5 = bf16[24,2,512,128]{3,2,1,0:T(8,128)(2,1)} copy(bf16[24,2,512,128]{3,2,1,0:T(8,128)(2,1)S(1)} %bitcast.1) | data formatting | bytes 12582912

commit v6 on v5

--- a/solution.py
+++ b/solution.py
@@ -152,7 +152,8 @@
             def _():
                 c_copy(j, span(t), 0).start()
 
-        b_copy(j, span(t)).start()
+        if t in (2, 4):
+            b_copy(j, pl.ds(0, 5) if t == 2 else pl.ds(5, 3)).start()
 
     def shared(j):
         dst = R.at[1 - c, j]
@@ -241,11 +242,10 @@
                     f(j, *args)
 
         on(i, (hop, 3))
-        on(i - 1, (product, 0, 1))
+        on(i - 1, (product, 0, 1), (product, 1, 0))
         on(i + 1, (hop, 1))
-        on(i - 1, (product, 1, 0))
+        on(i - 1, (product, 1, 1))
         on(i, (hop, 4))
-        on(i - 1, (product, 1, 1))
         on(i + 1, (hop, 2))
         on(i + 2, (hop, 0))
         on(i, (shared,), (product, 0, 0))

time: 110 us -> 110 us (level)
  no operation moved by 1% of the time
where the time goes in v6:
time: 110 us
  Pallas kernels  107 us (97%)
  local copies, waits for them, and re-layouts  2.71 us (2%)
    pallas_call x1, Pallas kernels, per_device(): pl.pallas_call(stack_kernel, out_shape=pltpu.VMEM((NX, BPC, parts, width,...  107 us
    unnamed x1, local copies, waits for them, and re-layouts  2.71 us

profile of v6, /device:TPU:1, one launch (start us, length us, event | category | flops | bytes accessed | tf_op | source)
XLA Modules:
  0.0 109.5 jit_solution(9576465142950603440)
XLA Ops:
  0.0 106.8 %stack.1 = bf16[4,6,2,512,128]{4,3,2,1,0:T(8,128)(2,1)S(1)} custom-call(s32[24]{0:T(128)} %bins_ref.1, s32[16]{0:T(128)} %mask_ref.1, bf16[16,2,128,512]{3,2,1,0:T(8,128)(2,1)} %spectra.1), custom_call_target="tpu_custom_call" | custom-call | flops 6442450944 | bytes 16777216 | tf_op jit(solution)/shard_map/stack/pallas_call | solution.py:288
  106.8 2.7 %copy.5 = bf16[24,2,512,128]{3,2,1,0:T(8,128)(2,1)} copy(bf16[24,2,512,128]{3,2,1,0:T(8,128)(2,1)S(1)} %bitcast.1) | data formatting | bytes 12582912
